TPU v7x, 256 devices: a whole 4x4x8 slice. The times are simulated.
256 devices in a mesh: gx: 8 (over z_hi, y), gy: 8 (over z_lo, core), gz: 4 (over x).
Axes of the slice: x: 4, y: 4, z: 8 (z_hi: 2, z_lo: 4; z = z_hi * 4 + z_lo), core: 2. Of those that a mesh axis runs over, the one named last changes fastest.
Arguments:
- charge: float32 [64, 128, 1024], P('gx', 'gy', 'gz'), may hold values from -6 to 6
- dielectric: float32 [64, 128, 1024], P('gx', 'gy', 'gz'), may hold values from 1 to 80
Outputs:
- potential: float32 [64, 128, 1024], P('gx', 'gy', 'gz')
All inputs are finite; a program needn't handle non-finite values.
Results may differ from a plain program's by a relative error of at most 0.0001.
Values sent between devices are 32-bit elements; how exact they have to be, the bound alone decides.
A program may use at most 64 MiB of HBM per device.

v0:
```python
import functools
import itertools
import math

import jax
import jax.numpy as jnp
from jax import lax
from jax.experimental import pallas as pl
from jax.experimental.pallas import tpu as pltpu
from jax.sharding import PartitionSpec as P

MESH = pl.DeviceIdType.MESH
F32 = jnp.float32
BF16 = jnp.bfloat16
OMEGA = 0.8
KEEP = 1.0 - OMEGA
FOURPI = 4.0 * math.pi
COARSE_SWEEPS = 8
NX, NY, NZ = 64, 128, 1024
GX, GY, GZ = 8, 8, 4
DIRS = [d for d in itertools.product((-1, 0, 1), repeat=3) if d != (0, 0, 0)]
ASIDE = [d for d in DIRS if d[0]]
LEVEL = [d for d in DIRS if not d[0]]
EDGES = [d for d in DIRS if 0 in d]
FLAT = [d for d in itertools.product((-1, 0, 1), repeat=2) if d != (0, 0)]


def loop(start, stop, body, init):
    return lax.fori_loop(start, stop, body, init, unroll=True)


def roll(values, shift, axis):
    return pltpu.roll(values, shift % values.shape[axis], axis)


def halves(values):
    high = values.astype(BF16)
    return high, (values - high.astype(F32)).astype(BF16)


def dot(a, b):
    if b.dtype == BF16:
        high, low = halves(a)
        return jnp.dot(high, b, preferred_element_type=F32) + jnp.dot(
            low, b, preferred_element_type=F32
        )
    high, low = halves(b)
    a = a.astype(BF16)
    return jnp.dot(a, high, preferred_element_type=F32) + jnp.dot(
        a, low, preferred_element_type=F32
    )


def place(index, own, size):
    half = (size - own) // 2
    return jnp.where(index < own + half, index, index - size)


def iota(shape, axis):
    return lax.broadcasted_iota(jnp.int32, shape, axis)


def restrict_z(own, size, out_own, out_size, weight):
    shape = (size, out_size)
    p = place(iota(shape, 0), own, size)
    q = place(iota(shape, 1), out_own, out_size)
    return jnp.where((p >> 1) == q, weight, 0.0).astype(BF16)


def pair_rows(groups, own, weight):
    shape = (groups * own // 2, groups * own)
    return jnp.where((iota(shape, 1) >> 1) == iota(shape, 0), weight, 0.0).astype(F32)


def spread(q, p):
    parent = p >> 1
    other = jnp.where((p & 1) == 0, parent - 1, parent + 1)
    return jnp.where(q == parent, 0.75, jnp.where(q == other, 0.25, 0.0)).astype(F32)


def prolong_z(own, size, out_own, out_size):
    shape = (size, out_size)
    weights = spread(place(iota(shape, 0), own, size), place(iota(shape, 1), out_own, out_size))
    return weights.astype(BF16)


def prolong_y(own, size, out_own, out_size):
    shape = (out_size, size)
    return spread(place(iota(shape, 1), own, size), place(iota(shape, 0), out_own, out_size))


def kernel(f_hbm, e_hbm, out, s):
    s = dict(zip(NAMES, s, strict=True))
    f_in, e_in = s["f_in"], s["e_in"]
    loads = [
        pltpu.make_async_copy(f_hbm, f_in, s["in_s"].at[0]),
        pltpu.make_async_copy(e_hbm, e_in, s["in_s"].at[1]),
    ]
    for load in loads:
        load.start()
    gx, gy, gz = (lax.axis_index(a) for a in ("gx", "gy", "gz"))
    core = gy & 1
    column = gx * 4 + (gy >> 1)
    has = [
        {-1: gx > 0, 0: True, 1: gx < GX - 1},
        {-1: gy > 0, 0: True, 1: gy < GY - 1},
        {-1: gz > 0, 0: True, 1: gz < GZ - 1},
    ]

    def there(d):
        found = [has[i][c] for i, c in enumerate(d) if c]
        return functools.reduce(jnp.logical_and, found)

    def peer(d):
        return (gx + d[0], gy + d[1], gz + (d[2] if len(d) > 2 else 0))

    def flip(d):
        return tuple(-c for c in d)

    sibling = (gx, gy + 1 - 2 * core, gz)

    barrier = pltpu.get_barrier_semaphore()

    def greet(device):
        pl.semaphore_signal(barrier, inc=1, device_id=device, device_id_type=MESH)

    order = sorted(DIRS, key=lambda d: (-abs(d[0]), abs(d[1]) + abs(d[2])))
    aside = [d for d in order if d[0]]
    for d in order:
        pl.when(there(d))(functools.partial(greet, peer(d)))

    def count(i):
        return 1 + has[i][-1].astype(jnp.int32) + has[i][1].astype(jnp.int32)

    lane128 = iota((16, 128), 1)
    row256 = iota((8, 256), 0)

    def mixed(side, x):
        f, e = f_in[x], e_in[x]
        if side == 0:
            return jnp.where(lane128 < 64, f[:, :128], roll(e[:, :128], 64, 1))
        return jnp.where(lane128 >= 64, f[:, 128:], roll(e[:, 128:], 64, 1))

    for load in loads:
        load.wait()
    share, part = lane128 >> 4, lane128 & 15
    share8 = iota((8, 128), 1) >> 4
    for zs in range(2):
        tile = jnp.zeros((16, 128), F32)
        lanes = slice(128 * zs, 128 * zs + 128)
        for x in range(8):
            f, e = f_in[x][:, lanes], e_in[x][:, lanes]
            f, e = roll(f, 16 * x + 8 * zs, 1), roll(e, 16 * x + 8 + 8 * zs, 1)
            tile = jnp.where(share == x, jnp.where(part < 8, f, e), tile)
        s["sz"][zs] = tile
    for ys in range(2):
        tiles = [jnp.zeros((8, 128), F32)] * 2
        for x in range(8):
            f, e = f_in[x], e_in[x]
            if ys == 0:
                rows = jnp.where(row256 < 4, f[:8], roll(e[:8], 4, 0))
            else:
                rows = jnp.where(row256 >= 4, f[8:], roll(e[8:], 4, 0))
            s["sy"][ys, x] = rows
            for zs in range(2):
                turned = roll(rows[:, 128 * zs : 128 * zs + 128], 16 * x + 16 * zs, 1)
                tiles[zs] = jnp.where(share8 == x, turned, tiles[zs])
        for zs in range(2):
            s["syz"][ys, zs] = tiles[zs]

    row8 = iota((8, 256), 0)
    for xs in range(2):
        one, two = (0, 1) if xs == 0 else (7, 6)
        near = slice(0, 1), slice(15, 16)
        s["ey"][xs, 0] = jnp.where(
            (row8 == 2) | (row8 == 3), roll(s["sy"][0, two], -2, 0), s["sy"][0, one]
        )
        s["ey"][xs, 1] = jnp.where(
            (row8 == 4) | (row8 == 5), roll(s["sy"][1, two], 2, 0), s["sy"][1, one]
        )
        s["ez"][xs, 0] = jnp.where(
            (lane128 >= 32) & (lane128 < 64), roll(mixed(0, two), -32, 1), mixed(0, one)
        )
        s["ez"][xs, 1] = jnp.where(
            (lane128 >= 64) & (lane128 < 96), roll(mixed(1, two), 32, 1), mixed(1, one)
        )
        for ys in range(2):
            s["ec"][xs, ys, 0] = e_in[one, near[ys], :128]
            s["ec"][xs, ys, 1] = e_in[one, near[ys], 128:]

    pl.semaphore_wait(barrier, count(0) * count(1) * count(2) - 1)

    def send(src, dst, name, index, device):
        return pltpu.make_async_remote_copy(
            src_ref=src,
            dst_ref=dst,
            send_sem=s[name + "_s"].at[index],
            recv_sem=s[name + "_r"].at[index],
            device_id=device,
            device_id_type=MESH,
        )

    def cut(dx, n, whole, base):
        if dx == 0:
            return pl.ds(0, whole), pl.ds(base, whole)
        if dx < 0:
            return pl.ds(0, n), pl.ds(base + whole, n)
        return pl.ds(whole - n, n), pl.ds(base - n, n)

    def round0(d):
        dx, dy, dz = d
        index = DIRS.index(d)
        xs, ys, zs = (int(c > 0) for c in d)
        if dy == 0 and dz == 0:
            a, b = cut(dx, 2, 8, 4)
            own = (pl.ds(0, 16), pl.ds(0, 256))
            first = send(f_in.at[a], s["f0"].at[(b, *own)], "c0", index, peer(d))
            a, b = cut(dx, 3, 8, 4)
            second = send(e_in.at[a], s["e0"].at[(b, *own)], "c0", 26 + (dx > 0), peer(d))
            return [first, second]
        if dx and dy and dz:
            source, target = s["ec"].at[xs, ys, zs], s["rec"].at[1 - xs, 1 - ys, 1 - zs]
        elif dx and dy:
            source, target = s["ey"].at[xs, ys], s["rey"].at[1 - xs, 1 - ys]
        elif dx:
            source, target = s["ez"].at[xs, zs], s["rez"].at[1 - xs, 1 - zs]
        elif dy and dz:
            source, target = s["syz"].at[ys, zs], s["ryz"].at[1 - ys, 1 - zs]
        elif dy:
            source, target = s["sy"].at[ys], s["ry"].at[1 - ys]
        else:
            source, target = s["sz"].at[zs], s["rz"].at[1 - zs]
        return [send(source, target, "c0", index, peer(d))]

    def iterate0(d):
        dx, dy, dz = d
        xs, ys, zs = (int(c > 0) for c in d)
        name = "v" + "x" * (dx != 0) + "y" * (dy != 0) + "z" * (dz != 0)
        slot = tuple(1 - i for i, c in zip((xs, ys, zs), d) if c)
        if dx and not dy:
            wide = 1 if dz else 2
            x = pl.ds(12 - wide if dx > 0 else 4, wide)
            lanes = pl.ds(128 * zs, 128) if dz else pl.ds(0, 256)
            source = s["b0"].at[x, pl.ds(0, 16), lanes]
        else:
            source = s["p" + name].at[tuple(1 - i for i in slot)]
        return [send(source, s[name].at[slot], "v0", EDGES.index(d), peer(d))]

    def pack_iterate0():
        row = iota((8, 256), 0)
        row_c = iota((8, 128), 0)
        for zs in range(2):
            tile = jnp.zeros((16, 128), F32)
            for k in range(8):
                v = s["b0"][4 + k, :16, 128 * zs : 128 * zs + 128]
                tile = jnp.where(share == k, roll(v, 16 * k + 16 * zs, 1), tile)
            s["pvz"][zs] = tile
        for ys in range(2):
            corner = jnp.zeros((8, 256), F32)
            tiles = [jnp.zeros((8, 256), F32)] * 2
            for k in range(8):
                v = s["b0"][4 + k, 8 * ys : 8 * ys + 8, :256]
                j = k & 3
                tiles[k >> 2] = jnp.where(
                    (row >> 1) == j, roll(v, 2 * j + 2 * ys, 0), tiles[k >> 2]
                )
                corner = jnp.where(row == k, roll(v, k + ys, 0), corner)
            s["pvy"][ys, 0], s["pvy"][ys, 1] = tiles
            s["pvyz"][ys, 0], s["pvyz"][ys, 1] = corner[:, :128], corner[:, 128:]
            near = slice(15, 16) if ys else slice(0, 1)
            s["pvxy"][0, ys] = s["b0"][4, near, :256]
            s["pvxy"][1, ys] = s["b0"][11, near, :256]

    def shrink(name, slab):
        width = slab(0).shape[1]
        row = iota((8, width), 0)
        for xs in range(2):
            one, two, three = (slab(k if xs == 0 else 3 - k) for k in range(3))
            tile = jnp.where(row >= 3, roll(two, 3, 0), one)
            s[name][xs, 0] = jnp.where(row >= 5, roll(three, 5, 0), tile)
            tile = jnp.where(row <= 4, roll(two, -3, 0), one)
            s[name][xs, 1] = jnp.where(row <= 2, roll(three, -5, 0), tile)

    def grow(tile, ys, distance):
        shift = (0, 3, 5)[distance - 1]
        return roll(tile, -shift if ys else shift, 0) if shift else tile

    def block1(name, wide):
        def copies(d):
            dx, dy, dz = d
            index = DIRS.index(d)
            if dx and dy:
                xs, ys = int(dx > 0), int(dy > 0)
                source, target = s["p" + name].at[xs, ys], s["r" + name].at[1 - xs, 1 - ys, 1 - dz]
                return [send(source, target, name, index, peer(d))]
            a, b = cut(dx, wide, 4, 4)
            own = pl.ds(4 + a.start, a.size)
            slot = (1 - dy) * 3 + 1 - dz
            buffer = s[name]
            return [send(buffer.at[4, own], buffer.at[slot, b], name, index, peer(d))]

        return copies

    def narrow1(d):
        dx, dy, dz = d
        xs, ys, zs = (int(c > 0) for c in d)
        if dy:
            source, target = s["ny"].at[xs, ys], s["rny"].at[1 - xs, 1 - ys, 1 - dz]
        elif dz:
            source, target = s["nz"].at[xs, zs], s["rnz"].at[1 - xs, 1 - zs]
        else:
            source, target = s["f1b"].at[4, pl.ds(6 if xs else 4, 2)], s["rn"].at[1 - xs]
        return [send(source, target, "n1", ASIDE.index(d), peer(d))]

    def flat1(d):
        dx, dy = d
        if dx and dy:
            xs, ys = int(dx > 0), int(dy > 0)
            source, target = s["pv1"].at[xs, ys], s["rv1"].at[1 - xs, 1 - ys]
            return [send(source, target, "v1", FLAT.index(d), peer(d))]
        a, b = cut(dx, 4, 4, 4)
        own = pl.ds(4 + a.start, a.size)
        return [send(s["v1"].at[1, own], s["v1"].at[1 - dy, b], "v1", FLAT.index(d), peer(d))]

    def start_all(dirs, copies):
        for d in dirs:

            @pl.when(there(d))
            def _(d=d):
                for copy in copies(d):
                    copy.start()

    def arrive_all(dirs, copies):
        for d in dirs:

            @pl.when(there(flip(d)))
            def _(d=d):
                for copy in copies(d):
                    copy.wait_recv()

    def leave_all(dirs, copies):
        for d in dirs:

            @pl.when(there(d))
            def _(d=d):
                for copy in copies(d):
                    copy.wait_send()

    def step_away(g, c, far):
        return (g + far * c >= 0) & (g + far * c < 8) if c else True

    def found(d, far):
        return jnp.logical_and(step_away(gx, d[0], far), step_away(gy, d[1], far))

    def tell(index, device):
        pl.semaphore_signal(s["tell"].at[index], inc=1, device_id=device, device_id_type=MESH)

    def tell_around(index, far):
        for d in FLAT:
            device = (gx + far * d[0], gy + far * d[1], gz)
            pl.when(found(d, far))(functools.partial(tell, index, device))

    def told_around(index, far):
        told = [found(d, far).astype(jnp.int32) for d in FLAT]
        pl.semaphore_wait(s["tell"].at[index], functools.reduce(jnp.add, told))

    def tell_plane():
        for device in ((gx ^ 4, gy, gz), (gx, gy ^ 4, gz), (gx ^ 4, gy ^ 4, gz)):
            tell(2, device)

    def all_told():
        pl.semaphore_wait(s["tell"].at[2], 3)

    far = 1 - (gx >> 2)

    def column_device(c):
        return (c >> 2, ((c & 3) << 1) + core, gz)

    def gather_start(name):
        mine = s[name].at[core, column]

        def one(k, carry):
            send(mine, mine, name, 1, column_device(16 * far + ((column + k) & 15))).start()
            return carry

        def other(k, carry):
            send(mine, mine, name, 0, column_device(16 * (1 - far) + ((column + k) & 15))).start()
            return carry

        lax.fori_loop(0, 16, one, 0)
        lax.fori_loop(1, 16, other, 0)

    def gathered(name, part):
        block = s[name].at[core, pl.ds(0, 15 + part)]
        return send(block, block, name, part, sibling)

    def handed(name, part, side):
        half = far if part else 1 - far
        block = s[name].at[side, pl.ds(16 * half, 16)]
        return send(block, block, name, 2 + part, sibling)

    start_all(order, round0)
    tell_around(0, 1)

    s["my1"][...] = pair_rows(2, 8, 0.5)
    s["mz1"][...] = restrict_z(128, 256, 64, 128, 1.0)
    s["my2"][...] = pair_rows(1, 32, 0.5)
    s["mz2"][...] = restrict_z(64, 128, 32, 128, 1.0)
    s["pz3"][...] = prolong_z(32, 128, 64, 128)
    s["py3"][...] = prolong_y(16, 16, 32, 32)
    s["pz2"][...] = prolong_z(64, 128, 128, 256)
    fine = place(iota((16, 32), 0), 8, 16) + 8 * gy
    s["py2"][...] = spread(iota((16, 32), 1), fine)
    s["pz1"][...] = prolong_z(128, 256, 256, 384)
    s["py1"][...] = prolong_y(8, 16, 16, 24)

    def inside(shape, own, index, total, axis):
        p = place(iota(shape, axis), own, shape[axis]) + own * index
        return (p >= 0) & (p < total)

    def x_inside(x, own, total):
        p = x + own * gx
        return (p >= 0) & (p < total)

    def mask(shape, own_y, own_z, total_y, total_z):
        return inside(shape, own_y, gy, total_y, 0) & inside(shape, own_z, gz, total_z, 1)

    def both(a, flag):
        return jnp.logical_and(a, jnp.broadcast_to(flag, a.shape))

    def beside(v, cx_low, cx, cy, cz, low, high):
        total = cx_low * low + cx * high
        total = total + cy * roll(v, -1, 0) + roll(cy * v, 1, 0)
        return total + cz * roll(v, -1, 1) + roll(cz * v, 1, 1)

    arrive_all(LEVEL, round0)
    told_around(0, 1)
    tell_around(1, 2)
    s["my0"][...] = pair_rows(4, 16, 0.5)
    s["mz0"][...] = restrict_z(256, 256, 128, 128, 1.0)
    for k in range(4):
        s["rs0"][16 * k : 16 * k + 16] = e_in[2 * k] + e_in[2 * k + 1]
    own_e1 = (dot(dot(s["my0"][...], s["rs0"][...]), s["mz0"][...]) * 0.25).reshape(4, 8, 128)
    s["e1"][4, 4:8] = own_e1
    shrink("pe1", lambda k: own_e1[k])
    start_all(order, block1("e1", 4))
    m0 = mask((24, 384), 16, 256, NY, NZ)
    ones0 = jnp.ones((24, 384), F32)
    low_lane = iota((16, 128), 1) < 64
    low_lane8 = iota((8, 128), 1) < 64
    low_row = iota((8, 256), 0) < 4
    low_row8 = iota((8, 128), 0) < 4

    def fill(x):
        m = both(m0, x_inside(x - 4, 8, NX))
        if 4 <= x < 12:
            distance, xs, f_own, e_own = 0, 0, f_in[x - 4], e_in[x - 4]
            k = x - 4
            y0, y1 = s["ry"][0, k], s["ry"][1, k]
            z0, z1 = s["rz"][0], s["rz"][1]
            f_z = jnp.where(low_lane, roll(z1, -16 * k, 1), roll(z0, -16 * k - 8, 1))
            e_z = jnp.where(low_lane, roll(z1, -16 * k - 8, 1), roll(z0, -16 * k - 16, 1))
        else:
            xs, distance = (0, 4 - x) if x < 4 else (1, x - 11)
            f_own, e_own = s["f0"][x, :16, :256], s["e0"][x, :16, :256]
            if distance == 3:
                e = jnp.concatenate([e_own, jnp.ones((16, 128), F32)], 1)
                e = jnp.concatenate([e, jnp.ones((8, 384), F32)], 0)
                s["e0"][x] = 1.0 / jnp.where(m, e, 1.0)
                return
            z0, z1, y0, y1 = s["rez"][xs, 0], s["rez"][xs, 1], s["rey"][xs, 0], s["rey"][xs, 1]
            if distance == 2:
                z0, z1, y0, y1 = roll(z0, -32, 1), roll(z1, 32, 1), roll(y0, -2, 0), roll(y1, 2, 0)
        if distance:
            f_z = jnp.where(low_lane, z1, z0)
            e_z = roll(jnp.where(low_lane, z0, z1), 64, 1)
        f_y = jnp.where(low_row, y1, y0)
        e_y = roll(jnp.where(low_row, y0, y1), 4, 0)
        f_c = jnp.zeros((8, 128), F32)
        e_c = jnp.ones((8, 128), F32)
        if distance == 0:
            c0, c1 = (
                jnp.where(
                    low_lane8,
                    roll(s["ryz"][i, 1], -16 * k, 1),
                    roll(s["ryz"][i, 0], -16 * k - 16, 1),
                )
                for i in range(2)
            )
            f_c = jnp.where(low_row8, c1, c0)
            e_c = roll(jnp.where(low_row8, c0, c1), 4, 0)
        elif distance == 1:
            c = s["rec"]
            c0 = jnp.where(low_lane8, c[xs, 0, 1], c[xs, 0, 0])
            c1 = jnp.where(low_lane8, c[xs, 1, 1], c[xs, 1, 0])
            e_c = jnp.where(low_row8, c1, c0)

        f, e = join(f_own, f_z, f_y, f_c), join(e_own, e_z, e_y, e_c)
        s["f0"][x] = jnp.where(m, f, 0.0) * FOURPI
        s["e0"][x] = 1.0 / jnp.where(m, e, 1.0)

    def join(own, z, y, c):
        top = jnp.concatenate([own, z], 1)
        return jnp.concatenate([top, jnp.concatenate([y, c], 1)], 0)

    def faces(here, after):
        return 2.0 / (here + after)

    def lateral(x):
        ic = s["e0"][x]
        cy, cz = faces(ic, roll(ic, -1, 0)), faces(ic, roll(ic, -1, 1))
        s["cy0"][x], s["cz0"][x] = cy, cz
        s["d0"][x] = cy + roll(cy, 1, 0) + cz + roll(cz, 1, 1)

    def along(x):
        s["cx0"][x] = faces(s["e0"][x], s["e0"][x + 1])

    def weigh(x):
        m = both(m0, x_inside(x - 4, 8, NX))
        diagonal = s["d0"][x] + s["cx0"][x] + s["cx0"][x - 1]
        weight = jnp.where(m, OMEGA / diagonal, 0.0)
        s["d0"][x], s["w0"][x] = diagonal, weight
        s["a0"][x] = weight * s["f0"][x]

    def total(level, src, x):
        c = str(level)
        v = s[src][x]
        return v, s["f" + c][x] + beside(
            v, s["cx" + c][x - 1], s["cx" + c][x], s["cy" + c][x], s["cz" + c][x],
            s[src][x - 1], s[src][x + 1],
        )

    def sweeps(level, src, dst, start, stop):
        def one(x, carry):
            v, u = total(level, src, x)
            s[dst][x] = KEEP * v + s[f"w{level}"][x] * u
            return carry

        loop(start, stop, one, 0)

    def residue(level, src, x):
        v, u = total(level, src, x)
        return u - s[f"d{level}"][x] * v

    for x in range(4, 12):
        fill(x)
        lateral(x)
    for x in range(4, 11):
        along(x)
    for x in range(5, 11):
        weigh(x)
    sweeps(0, "a0", "b0", 6, 10)

    arrive_all(aside, round0)
    told_around(1, 2)
    tell_plane()
    for x in (1, 2, 3, 12, 13, 14):
        fill(x)
    for x in (2, 3, 12, 13):
        lateral(x)
    for x in (1, 2, 3, 11, 12, 13):
        along(x)
    for x in (2, 3, 4, 11, 12, 13):
        weigh(x)
    sweeps(0, "a0", "b0", 3, 6)
    sweeps(0, "a0", "b0", 10, 13)

    def pairs0(k, carry):
        r = residue(0, "b0", 4 + 2 * k) + residue(0, "b0", 5 + 2 * k)
        s["rs0"][pl.ds(pl.multiple_of(k * 16, 16), 16)] = r[:16, :256]
        return carry

    loop(0, 4, pairs0, 0)
    own_f1 = dot(dot(s["my0"][...], s["rs0"][...]), s["mz0"][...]).reshape(4, 8, 128)
    s["f1b"][4, 4:8] = own_f1
    lane8 = iota((8, 128), 1)
    for xs in range(2):
        one, two = (own_f1[0], own_f1[1]) if xs == 0 else (own_f1[3], own_f1[2])
        two = roll(two, 64, 1)
        s["nz"][xs, 0] = jnp.where(lane8 < 64, one, two)
        s["nz"][xs, 1] = jnp.where(lane8 >= 64, one, two)
        s["ny"][xs, 0], s["ny"][xs, 1] = one[0:1], one[7:8]
    start_all(aside, narrow1)
    start_all(LEVEL, block1("f1b", 3))
    shrink("pf1b", lambda k: own_f1[k])
    start_all(aside, block1("f1b", 3))
    pack_iterate0()
    start_all(EDGES, iterate0)

    def coefficients(ie, x, m, ic, cx_low):
        inext = ie[x + 1]
        cx = 2.0 / (ic + inext)
        cy = 2.0 / (ic + roll(ic, -1, 0))
        cz = 2.0 / (ic + roll(ic, -1, 1))
        diagonal = cx + cx_low + cy + roll(cy, 1, 0) + cz + roll(cz, 1, 1)
        weight = jnp.where(m, OMEGA / diagonal, 0.0)
        return inext, cx, cy, cz, diagonal, weight

    m1 = mask((16, 256), 8, 128, NY // 2, NZ // 2)

    def join1(name, x, other, reach):
        b = s[name]
        distance = 4 - x if x < 4 else x - 7 if x > 7 else 0

        def across(y):
            tiles = [b[y * 3 + i, x] for i in range(3)]
            if distance and y != 1:
                r, xs, ys = s["r" + name], int(x > 7), int(y == 2)
                tiles = [grow(r[xs, ys, i], ys, distance) for i in range(3)]
            return jnp.concatenate([tiles[1], jnp.where(low_lane8, tiles[2], tiles[0])], 1)

        under = jnp.full((8, 256), other, F32)
        if distance < reach:
            under = jnp.where(low_row, across(2), across(0))
        both_rows = jnp.concatenate([across(1), under], 0)
        return jnp.where(both(m1, x_inside(x - 4, 4, NX // 2)), both_rows, other)

    arrive_all(order, block1("e1", 4))
    for x in range(12):
        e = join1("e1", x, 1.0, 4)
        s["ie1"][x] = 1.0 / e
        if 4 <= x < 8:
            half = (x - 4) // 2 * 8
            if x % 2 == 0:
                s["rs1"][half : half + 8] = e[:8]
            else:
                s["rs1"][half : half + 8] += e[:8]
    s["ge"][core, column] = dot(dot(s["my1"][...], s["rs1"][...]), s["mz1"][...]) * 0.25
    all_told()
    gather_start("ge")
    s["cx1"][0] = 2.0 / (s["ie1"][0] + s["ie1"][1])

    def make1(x, carry):
        ic, cx_low = carry
        m = both(m1, x_inside(x - 4, 4, NX // 2))
        ic, cx, cy, cz, diagonal, weight = coefficients(s["ie1"], x, m, ic, cx_low)
        s["cx1"][x], s["cy1"][x], s["cz1"][x] = cx, cy, cz
        s["d1"][x], s["w1"][x] = diagonal, weight
        return ic, cx

    loop(1, 11, make1, (s["ie1"][1], s["cx1"][0]))

    def beside1(x):
        xs, distance = (0, 4 - x) if x < 4 else (1, x - 7)
        own = s["rn"][xs, distance - 1 if xs else 2 - distance]
        z0, z1 = s["rnz"][xs, 0], s["rnz"][xs, 1]
        around = jnp.where(low_lane8, z1, z0)
        under = jnp.zeros((8, 256), F32)
        if distance == 2:
            around = roll(jnp.where(low_lane8, z0, z1), 64, 1)
        else:
            r = s["rny"]
            rows = [
                jnp.where(low_row8, r[xs, 1, i], r[xs, 0, i]) for i in range(3)
            ]
            under = jnp.concatenate([rows[1], jnp.where(low_lane8, rows[2], rows[0])], 1)
        values = jnp.concatenate([jnp.concatenate([own, around], 1), under], 0)
        return jnp.where(both(m1, x_inside(x - 4, 4, NX // 2)), values, 0.0)

    arrive_all(LEVEL, block1("f1b", 3))
    for x in range(4, 8):
        s["f1"][x] = join1("f1b", x, 0.0, 3)
        s["a1"][x] = s["w1"][x] * s["f1"][x]
    arrive_all(aside, narrow1)
    for x in (2, 3, 8, 9):
        f = beside1(x)
        s["f1"][x] = f
        s["a1"][x] = s["w1"][x] * f
    sweeps(1, "a1", "b1", 3, 9)
    for k in range(2):
        r = residue(1, "b1", 4 + 2 * k) + residue(1, "b1", 5 + 2 * k)
        s["rs1"][8 * k : 8 * k + 8] = r[:8]
    s["gf"][core, column] = dot(dot(s["my1"][...], s["rs1"][...]), s["mz1"][...])
    gather_start("gf")
    for x in range(4, 8):
        s["v1"][1, x] = s["b1"][x, :8]
    shrink("pv1", lambda k: s["v1"][1, 4 + k])
    start_all(FLAT, flat1)

    row8 = iota((8, 128), 0) < 4

    def arrange(name, half, write):
        def one(k, carry):
            k = 16 * half + k
            even, odd = s[name][0, k], s[name][1, k]
            x = 2 * (k >> 2)
            rows = pl.ds(pl.multiple_of((k & 3) * 8, 8), 8)
            write(x + 4, rows, jnp.where(row8, even, roll(odd, 4, 0)))
            write(x + 5, rows, jnp.where(row8, roll(even, 4, 0), odd))
            return carry

        loop(0, 16, one, 0)

    def collect(name, write):
        for part in range(2):
            gathered(name, part).wait_recv()
            handed(name, part, core).start()
        for part in range(2):
            handed(name, part, 1 - core).wait_recv()
            arrange(name, far if part else 1 - far, write)

    def put_e2(x, rows, values):
        s["e2"][x, rows] = values
        s["ie2"][x, rows] = 1.0 / values

    collect("ge", put_e2)
    shape2 = (32, 128)
    last2, first2 = iota(shape2, 0) == 31, iota(shape2, 0) == 0
    in_z2 = inside(shape2, 64, gz, NZ // 4, 1)
    s["ie2"][3] = jnp.ones(shape2, F32)
    s["ie2"][20] = jnp.ones(shape2, F32)

    def edge_faces(ic, first, last):
        cy = 2.0 / (ic + jnp.where(last, 1.0, roll(ic, -1, 0)))
        below = jnp.where(first, 2.0 / (ic + 1.0), roll(cy, 1, 0))
        return cy, below

    s["cx2"][3] = 2.0 / (1.0 + s["ie2"][4])

    def make2(x, carry):
        ic, cx_low = carry
        inext = s["ie2"][x + 1]
        cx = 2.0 / (ic + inext)
        cy, below = edge_faces(ic, first2, last2)
        cz = 2.0 / (ic + roll(ic, -1, 1))
        diagonal = cx + cx_low + cy + below + cz + roll(cz, 1, 1)
        s["cx2"][x], s["cz2"][x] = cx, cz
        s["cy2"][x] = jnp.where(last2, 0.0, cy)
        s["d2"][x] = diagonal
        s["w2"][x] = jnp.where(in_z2, OMEGA / diagonal, 0.0)
        return inext, cx

    loop(4, 20, make2, (s["ie2"][4], s["cx2"][3]))
    for x in range(4):
        for name in ("a2", "b2"):
            s[name][x] = jnp.zeros(shape2, F32)
            s[name][20 + x] = jnp.zeros(shape2, F32)

    def down3(pair):
        def one(k, carry):
            rows = pl.ds(pl.multiple_of(k * 16, 16), 16)
            s["rs3"][rows] = dot(s["my2"][...], pair(k))
            return carry

        loop(0, 8, one, 0)
        return dot(s["rs3"][...], s["mz2"][...]).reshape(8, 16, 128)

    shape3 = (8, 16, 128)
    p3 = place(iota(shape3, 2), 32, 128)
    near3 = (p3 >= -16) & (p3 < 48)
    e3 = down3(lambda k: s["e2"][4 + 2 * k] + s["e2"][5 + 2 * k]) * 0.25
    ie3 = 1.0 / jnp.where(near3, e3, 1.0)
    first3, last3 = iota(shape3, 1) == 0, iota(shape3, 1) == 15
    edge = jnp.ones((1, 16, 128), F32)
    none = jnp.zeros((1, 16, 128), F32)

    def roll3(values, shift, axis):
        return roll(values.reshape(128, 128), shift, 1).reshape(shape3) if axis == 2 else jnp.stack(
            [roll(values[k], shift, 0) for k in range(8)]
        )

    around = jnp.concatenate([edge, ie3, edge], 0)
    cx3 = 2.0 / (around[1:] + around[:-1])
    cy3 = 2.0 / (ie3 + jnp.where(last3, 1.0, roll3(ie3, -1, 1)))
    below3 = jnp.where(first3, 2.0 / (ie3 + 1.0), roll3(cy3, 1, 1))
    cz3 = 2.0 / (ie3 + roll3(ie3, -1, 2))
    d3 = cx3[1:] + cx3[:-1] + cy3 + below3 + cz3 + roll3(cz3, 1, 2)
    q3 = p3 + 32 * gz
    s["w3"][...] = jnp.where((q3 >= 0) & (q3 < NZ // 8), OMEGA / d3, 0.0)
    s["cx3"][...] = cx3
    s["cy3"][...] = jnp.where(last3, 0.0, cy3)
    s["cz3"][...] = cz3

    leave_all(order, round0)
    leave_all(order, block1("e1", 4))
    leave_all(aside, narrow1)
    leave_all(LEVEL, block1("f1b", 3))
    def put_f2(x, rows, values):
        s["f2"][x, rows] = values
        s["a2"][x, rows] = s["w2"][x, rows] * values

    collect("gf", put_f2)
    sweeps(2, "a2", "b2", 4, 20)
    f3 = down3(lambda k: residue(2, "b2", 4 + 2 * k) + residue(2, "b2", 5 + 2 * k))
    s["f3"][...] = f3

    def coarse(_, v):
        cx, cy, cz = s["cx3"][...], s["cy3"][...], s["cz3"][...]
        after = jnp.concatenate([v[1:], none], 0)
        before = jnp.concatenate([none, v[:-1]], 0)
        u = s["f3"][...] + cx[1:] * after + cx[:-1] * before
        u = u + cy * roll3(v, -1, 1) + roll3(cy * v, 1, 1)
        u = u + cz * roll3(v, -1, 2) + roll3(cz * v, 1, 2)
        return KEEP * v + s["w3"][...] * u

    v3 = loop(0, COARSE_SWEEPS - 1, coarse, s["w3"][...] * f3)

    wide = dot(v3.reshape(128, 128), s["pz3"][...]).reshape(8, 16, 128)
    rows3 = [dot(s["py3"][...], wide[k]) for k in range(8)]
    nothing = jnp.zeros(shape2, F32)
    for k in range(8):
        low = rows3[k - 1] if k else nothing
        high = rows3[k + 1] if k < 7 else nothing
        for i, other in ((0, low), (1, high)):
            x = 4 + 2 * k + i
            add = 0.75 * rows3[k] + 0.25 * other
            s["b2"][x] += jnp.where(in_z2, add, 0.0)
    sweeps(2, "b2", "a2", 4, 20)
    sweeps(2, "a2", "b2", 4, 20)

    for k in range(8):
        s["up1"][16 * k : 16 * k + 16] = dot(s["py2"][...], s["b2"][2 * gx + 1 + k])
    up1 = dot(s["up1"][...], s["pz2"][...])
    arrive_all(FLAT, flat1)
    arrive_all(aside, block1("f1b", 3))
    for x in (1, 2, 3, 8, 9, 10):
        s["f1"][x] = join1("f1b", x, 0.0, 3)
    up1 = up1.reshape(8, 16, 256)
    for x in range(12):
        k = (x - 4) // 2 + 3
        other = up1[k - 1] if x % 2 == 0 else up1[k + 1]
        add = 0.75 * up1[k] + 0.25 * other
        distance = 4 - x if x < 4 else x - 7 if x > 7 else 0
        under = jnp.zeros((8, 256), F32)
        if distance == 0:
            under = jnp.where(low_row, s["v1"][2, x], s["v1"][0, x])
        elif distance < 4:
            r = s["rv1"]
            after, before = (grow(r[int(x > 7), ys], ys, distance) for ys in (1, 0))
            under = jnp.where(low_row, after, before)
        v = jnp.concatenate([s["v1"][1, x], under], 0) + add
        s["a1"][x] = jnp.where(both(m1, x_inside(x - 4, 4, NX // 2)), v, 0.0)
    sweeps(1, "a1", "b1", 1, 11)
    sweeps(1, "b1", "a1", 2, 10)

    arrive_all(EDGES, iterate0)

    def whole0(x):
        nothing = [jnp.zeros(shape, F32) for shape in ((16, 128), (8, 256), (8, 128))]
        if 4 <= x < 12:
            k = x - 4
            z = jnp.where(
                low_lane, roll(s["vz"][1], -16 * k, 1), roll(s["vz"][0], -16 * k - 16, 1)
            )
            i, j = k >> 2, 2 * (k & 3)
            y = jnp.where(
                low_row, roll(s["vy"][1, i], -j, 0), roll(s["vy"][0, i], -j - 2, 0)
            )
            c = [jnp.where(low_lane8, s["vyz"][i, 1], s["vyz"][i, 0]) for i in range(2)]
            c = [roll(c[0], -k - 1, 0), roll(c[1], -k, 0)]
            return join(s["b0"][x, :16, :256], z, y, jnp.where(low_row8, c[1], c[0]))
        xs, distance = (0, 4 - x) if x < 4 else (1, x - 11)
        own = s["vx"][xs, 2 - distance if xs == 0 else distance - 1]
        if distance == 2:
            return join(own, *nothing)
        z = jnp.where(low_lane, s["vxz"][xs, 1, 0], s["vxz"][xs, 0, 0])
        y = jnp.where(low_row, s["vxy"][xs, 1], s["vxy"][xs, 0])
        return join(own, z, y, nothing[2])

    for k in range(8):
        s["up0"][24 * k : 24 * k + 24] = dot(s["py1"][...], s["a1"][2 + k])
    up0 = dot(s["up0"][...], s["pz1"][...]).reshape(8, 24, 384)
    for x in range(2, 14):
        k = (x - 4) // 2 + 2
        other = up0[k - 1] if x % 2 == 0 else up0[k + 1]
        add = 0.75 * up0[k] + 0.25 * other
        v = whole0(x) + add
        s["a0"][x] = jnp.where(both(m0, x_inside(x - 4, 8, NX)), v, 0.0)
    sweeps(0, "a0", "g0", 3, 13)

    def finish(x, carry):
        v, u = total(0, "g0", x)
        out[x - 4] = (KEEP * v + s["w0"][x] * u)[:16, :256]
        return carry

    loop(4, 12, finish, 0)

    leave_all(aside, block1("f1b", 3))
    leave_all(FLAT, flat1)
    leave_all(EDGES, iterate0)
    for name in ("ge", "gf"):
        for part in range(2):
            gathered(name, 1 - part).wait_send()
            handed(name, part, core).wait_send()


def buffers():
    def vmem(*shape):
        return pltpu.VMEM(shape, F32)

    def half(*shape):
        return pltpu.VMEM(shape, BF16)

    table = {
        "sz": vmem(2, 16, 128), "rz": vmem(2, 16, 128),
        "sy": vmem(2, 8, 8, 256), "ry": vmem(2, 8, 8, 256),
        "syz": vmem(2, 2, 8, 128), "ryz": vmem(2, 2, 8, 128),
        "ey": vmem(2, 2, 8, 256), "rey": vmem(2, 2, 8, 256),
        "ez": vmem(2, 2, 16, 128), "rez": vmem(2, 2, 16, 128),
        "ec": vmem(2, 2, 2, 1, 128), "rec": vmem(2, 2, 2, 1, 128),
        "vx": vmem(2, 2, 16, 256), "vy": vmem(2, 2, 8, 256), "vz": vmem(2, 16, 128),
        "pvy": vmem(2, 2, 8, 256), "pvz": vmem(2, 16, 128), "pvxy": vmem(2, 2, 1, 256),
        "vxy": vmem(2, 2, 1, 256), "vxz": vmem(2, 2, 1, 16, 128), "vyz": vmem(2, 2, 8, 128),
        "pvyz": vmem(2, 2, 8, 128),
        "pe1": vmem(2, 2, 8, 128), "re1": vmem(2, 2, 3, 8, 128),
        "ny": vmem(2, 2, 1, 128), "rny": vmem(2, 2, 3, 1, 128),
        "nz": vmem(2, 2, 8, 128), "rnz": vmem(2, 2, 8, 128), "rn": vmem(2, 2, 8, 128),
        "pf1b": vmem(2, 2, 8, 128), "rf1b": vmem(2, 2, 3, 8, 128),
        "pv1": vmem(2, 2, 8, 256), "rv1": vmem(2, 2, 8, 256), "g0": vmem(16, 24, 384),
        "e1": vmem(9, 12, 8, 128), "f1b": vmem(9, 12, 8, 128), "v1": vmem(3, 12, 8, 256),
        "ge": vmem(2, 32, 8, 128), "gf": vmem(2, 32, 8, 128),
        "my0": vmem(32, 64), "mz0": half(256, 128), "my1": vmem(8, 16), "mz1": half(256, 128),
        "my2": vmem(16, 32), "mz2": half(128, 128), "pz3": half(128, 128), "py3": vmem(32, 16),
        "pz2": half(128, 256), "py2": vmem(16, 32), "pz1": half(256, 384), "py1": vmem(24, 16),
        "rs0": vmem(64, 256), "rs1": vmem(16, 256), "rs3": vmem(128, 128),
        "up1": vmem(128, 128), "up0": vmem(192, 256),
        "ie1": vmem(12, 16, 256), "e2": vmem(24, 32, 128), "ie2": vmem(24, 32, 128),
        "f3": vmem(8, 16, 128), "w3": vmem(8, 16, 128), "cx3": vmem(9, 16, 128),
        "cy3": vmem(8, 16, 128), "cz3": vmem(8, 16, 128),
    }
    shapes = {"0": (16, 24, 384), "1": (12, 16, 256), "2": (24, 32, 128)}
    for level, shape in shapes.items():
        for name in ("f", "cx", "cy", "cz", "d", "w", "a", "b"):
            table[name + level] = vmem(*shape)
    table["f_in"], table["e_in"] = vmem(8, 16, 256), vmem(8, 16, 256)
    table["tell"] = pltpu.SemaphoreType.REGULAR((3,))
    table["in_s"] = pltpu.SemaphoreType.DMA((2,))
    table["e0"] = vmem(16, 24, 384)
    for name, number in (("c0", 28), ("v0", 18), ("n1", 18), ("e1", 26), ("f1b", 26), ("v1", 8), ("ge", 4), ("gf", 4)):
        table[name + "_s"] = pltpu.SemaphoreType.DMA((number,))
        table[name + "_r"] = pltpu.SemaphoreType.DMA((number,))
    return table


NAMES = list(buffers())


def on_device(charge, dielectric):
    return pl.pallas_call(
        lambda f, e, o, *s: kernel(f, e, o, s),
        out_shape=jax.ShapeDtypeStruct((8, 16, 256), F32),
        in_specs=[pl.BlockSpec(memory_space=pltpu.HBM)] * 2,
        out_specs=pl.BlockSpec(memory_space=pltpu.VMEM),
        scratch_shapes=list(buffers().values()),
        compiler_params=pltpu.CompilerParams(
            collective_id=0, has_side_effects=True, vmem_limit_bytes=60 * 2**20
        ),
    )(charge, dielectric)


def solution(mesh):
    placed = (P("gx", "gy", "gz"), P("gx", "gy", "gz"))
    return jax.shard_map(
        on_device, mesh=mesh, in_specs=placed, out_specs=P("gx", "gy", "gz"), check_vma=False
    )
```

profile of v0, /device:TPU:59, one launch (start us, length us, event | category | flops | bytes accessed | tf_op | source)
XLA Modules:
  0.0 45.0 jit_solution(10391289790618944106)
XLA Ops:
  0.0 43.5 %shard_map.28 = f32[8,16,256]{2,1,0:T(8,128)} custom-call(f32[8,16,256]{2,1,0:T(8,128)} %f.1, f32[8,16,256]{2,1,0:T(8,128)} %e.1), custom_call_target="tpu_custom_call" | custom-call | tf_op jit(solution)/shard_map/pallas_call | solution.py:939
  43.5 1.6 %copy.4 = f32[8,16,256]{2,1,0:T(8,128)} copy(f32[8,16,256]{2,1,0:T(8,128)} %shard_map.28) | data formatting | bytes 262144
where the time goes:
time: 45.2 us; the launch traced here: 45 us
  Pallas kernels  43.5 us (96%)
  local copies, waits for them, and re-layouts  1.57 us (3%)
    pallas_call x1, Pallas kernels, on_device(): pl.pallas_call(lambda f, e, o, *s: kernel(f, e, o, s), out_shape=jax.Shap...  43.5 us
    unnamed x1, local copies, waits for them, and re-layouts  1.57 us

commit v1 on v0

--- a/solution.py
+++ b/solution.py
@@ -143,7 +143,7 @@
 
     for load in loads:
         load.wait()
-    share, part = lane128 >> 4, lane128 & 15
+    share, within = lane128 >> 4, lane128 & 15
     share8 = iota((8, 128), 1) >> 4
     for zs in range(2):
         tile = jnp.zeros((16, 128), F32)
@@ -151,7 +151,7 @@
         for x in range(8):
             f, e = f_in[x][:, lanes], e_in[x][:, lanes]
             f, e = roll(f, 16 * x + 8 * zs, 1), roll(e, 16 * x + 8 + 8 * zs, 1)
-            tile = jnp.where(share == x, jnp.where(part < 8, f, e), tile)
+            tile = jnp.where(share == x, jnp.where(within < 8, f, e), tile)
         s["sz"][zs] = tile
     for ys in range(2):
         tiles = [jnp.zeros((8, 128), F32)] * 2
@@ -285,6 +285,19 @@
         shift = (0, 3, 5)[distance - 1]
         return roll(tile, -shift if ys else shift, 0) if shift else tile
 
+    def pair(name, slab):
+        half = iota((8, slab(0).shape[1]), 0) >= 4
+        for xs in range(2):
+            from_edge = [slab(k if xs == 0 else 3 - k) for k in range(4)]
+            for t in range(2):
+                one, two = from_edge[2 * t], roll(from_edge[2 * t + 1], 4, 0)
+                s[name][xs, 0, t] = jnp.where(half, two, one)
+                s[name][xs, 1, t] = jnp.where(half, one, two)
+
+    def part(tiles, distance):
+        tile = tiles[(distance - 1) >> 1]
+        return tile if distance & 1 else roll(tile, 4, 0)
+
     def block1(name, wide):
         def copies(d):
             dx, dy, dz = d
@@ -442,7 +455,7 @@
         s["rs0"][16 * k : 16 * k + 16] = e_in[2 * k] + e_in[2 * k + 1]
     own_e1 = (dot(dot(s["my0"][...], s["rs0"][...]), s["mz0"][...]) * 0.25).reshape(4, 8, 128)
     s["e1"][4, 4:8] = own_e1
-    shrink("pe1", lambda k: own_e1[k])
+    pair("pe1", lambda k: own_e1[k])
     start_all(order, block1("e1", 4))
     m0 = mask((24, 384), 16, 256, NY, NZ)
     ones0 = jnp.ones((24, 384), F32)
@@ -606,7 +619,10 @@
             tiles = [b[y * 3 + i, x] for i in range(3)]
             if distance and y != 1:
                 r, xs, ys = s["r" + name], int(x > 7), int(y == 2)
-                tiles = [grow(r[xs, ys, i], ys, distance) for i in range(3)]
+                if name == "e1":
+                    tiles = [part(r[xs, ys, i], distance) for i in range(3)]
+                else:
+                    tiles = [grow(r[xs, ys, i], ys, distance) for i in range(3)]
             return jnp.concatenate([tiles[1], jnp.where(low_lane8, tiles[2], tiles[0])], 1)
 
         under = jnp.full((8, 256), other, F32)
@@ -617,7 +633,7 @@
 
     arrive_all(order, block1("e1", 4))
     for x in range(12):
-        e = join1("e1", x, 1.0, 4)
+        e = join1("e1", x, 1.0, 5)
         s["ie1"][x] = 1.0 / e
         if 4 <= x < 8:
             half = (x - 4) // 2 * 8
@@ -659,7 +675,7 @@
 
     arrive_all(LEVEL, block1("f1b", 3))
     for x in range(4, 8):
-        s["f1"][x] = join1("f1b", x, 0.0, 3)
+        s["f1"][x] = join1("f1b", x, 0.0, 4)
         s["a1"][x] = s["w1"][x] * s["f1"][x]
     arrive_all(aside, narrow1)
     for x in (2, 3, 8, 9):
@@ -674,7 +690,7 @@
     gather_start("gf")
     for x in range(4, 8):
         s["v1"][1, x] = s["b1"][x, :8]
-    shrink("pv1", lambda k: s["v1"][1, 4 + k])
+    pair("pv1", lambda k: s["v1"][1, 4 + k])
     start_all(FLAT, flat1)
 
     row8 = iota((8, 128), 0) < 4
@@ -814,19 +830,18 @@
     arrive_all(FLAT, flat1)
     arrive_all(aside, block1("f1b", 3))
     for x in (1, 2, 3, 8, 9, 10):
-        s["f1"][x] = join1("f1b", x, 0.0, 3)
+        s["f1"][x] = join1("f1b", x, 0.0, 4)
     up1 = up1.reshape(8, 16, 256)
     for x in range(12):
         k = (x - 4) // 2 + 3
         other = up1[k - 1] if x % 2 == 0 else up1[k + 1]
         add = 0.75 * up1[k] + 0.25 * other
         distance = 4 - x if x < 4 else x - 7 if x > 7 else 0
-        under = jnp.zeros((8, 256), F32)
         if distance == 0:
             under = jnp.where(low_row, s["v1"][2, x], s["v1"][0, x])
-        elif distance < 4:
+        else:
             r = s["rv1"]
-            after, before = (grow(r[int(x > 7), ys], ys, distance) for ys in (1, 0))
+            after, before = (part(r[int(x > 7), ys], distance) for ys in (1, 0))
             under = jnp.where(low_row, after, before)
         v = jnp.concatenate([s["v1"][1, x], under], 0) + add
         s["a1"][x] = jnp.where(both(m1, x_inside(x - 4, 4, NX // 2)), v, 0.0)
@@ -902,11 +917,11 @@
         "pvy": vmem(2, 2, 8, 256), "pvz": vmem(2, 16, 128), "pvxy": vmem(2, 2, 1, 256),
         "vxy": vmem(2, 2, 1, 256), "vxz": vmem(2, 2, 1, 16, 128), "vyz": vmem(2, 2, 8, 128),
         "pvyz": vmem(2, 2, 8, 128),
-        "pe1": vmem(2, 2, 8, 128), "re1": vmem(2, 2, 3, 8, 128),
+        "pe1": vmem(2, 2, 2, 8, 128), "re1": vmem(2, 2, 3, 2, 8, 128),
         "ny": vmem(2, 2, 1, 128), "rny": vmem(2, 2, 3, 1, 128),
         "nz": vmem(2, 2, 8, 128), "rnz": vmem(2, 2, 8, 128), "rn": vmem(2, 2, 8, 128),
         "pf1b": vmem(2, 2, 8, 128), "rf1b": vmem(2, 2, 3, 8, 128),
-        "pv1": vmem(2, 2, 8, 256), "rv1": vmem(2, 2, 8, 256), "g0": vmem(16, 24, 384),
+        "pv1": vmem(2, 2, 2, 8, 256), "rv1": vmem(2, 2, 2, 8, 256), "g0": vmem(16, 24, 384),
         "e1": vmem(9, 12, 8, 128), "f1b": vmem(9, 12, 8, 128), "v1": vmem(3, 12, 8, 256),
         "ge": vmem(2, 32, 8, 128), "gf": vmem(2, 32, 8, 128),
         "my0": vmem(32, 64), "mz0": half(256, 128), "my1": vmem(8, 16), "mz1": half(256, 128),

time: 45.2 us -> 46.1 us (1.020)
    pallas_call x1, Pallas kernels: 43.5 us -> 43.9 us  [on_device(): pl.pallas_call(lambda f, e, o, *s: kernel(f, e, o, s), out_shape=jax.Shap...]
where the time goes in v1:
time: 46.1 us; the launch traced here: 45.5 us
  Pallas kernels  43.9 us (95%)
  local copies, waits for them, and re-layouts  1.57 us (3%)
    pallas_call x1, Pallas kernels, on_device(): pl.pallas_call(lambda f, e, o, *s: kernel(f, e, o, s), out_shape=jax.Shap...  43.9 us
    unnamed x1, local copies, waits for them, and re-layouts  1.57 us

profile of v1, /device:TPU:59, one launch (start us, length us, event | category | flops | bytes accessed | tf_op | source)
XLA Modules:
  0.0 45.5 jit_solution(258401800676789354)
XLA Ops:
  0.0 43.9 %shard_map.28 = f32[8,16,256]{2,1,0:T(8,128)} custom-call(f32[8,16,256]{2,1,0:T(8,128)} %f.1, f32[8,16,256]{2,1,0:T(8,128)} %e.1), custom_call_target="tpu_custom_call" | custom-call | tf_op jit(solution)/shard_map/pallas_call | solution.py:954
  44.0 1.6 %copy.4 = f32[8,16,256]{2,1,0:T(8,128)} copy(f32[8,16,256]{2,1,0:T(8,128)} %shard_map.28) | data formatting | bytes 262144

commit v2 on v1

--- a/solution.py
+++ b/solution.py
@@ -456,7 +456,7 @@
     own_e1 = (dot(dot(s["my0"][...], s["rs0"][...]), s["mz0"][...]) * 0.25).reshape(4, 8, 128)
     s["e1"][4, 4:8] = own_e1
     pair("pe1", lambda k: own_e1[k])
-    start_all(order, block1("e1", 4))
+    start_all(LEVEL, block1("e1", 4))
     m0 = mask((24, 384), 16, 256, NY, NZ)
     ones0 = jnp.ones((24, 384), F32)
     low_lane = iota((16, 128), 1) < 64
@@ -564,6 +564,7 @@
         weigh(x)
     sweeps(0, "a0", "b0", 6, 10)
 
+    start_all(aside, block1("e1", 4))
     arrive_all(aside, round0)
     told_around(1, 2)
     tell_plane()
@@ -595,10 +596,10 @@
         s["ny"][xs, 0], s["ny"][xs, 1] = one[0:1], one[7:8]
     start_all(aside, narrow1)
     start_all(LEVEL, block1("f1b", 3))
+    pack_iterate0()
+    start_all(EDGES, iterate0)
     shrink("pf1b", lambda k: own_f1[k])
     start_all(aside, block1("f1b", 3))
-    pack_iterate0()
-    start_all(EDGES, iterate0)
 
     def coefficients(ie, x, m, ic, cx_low):
         inext = ie[x + 1]

time: 46.1 us -> 45.8 us (level)
  Pallas kernels: 43.9 us -> 43.3 us
    pallas_call x1, Pallas kernels: 43.9 us -> 43.3 us  [on_device(): pl.pallas_call(lambda f, e, o, *s: kernel(f, e, o, s), out_shape=jax.Shap...]
where the time goes in v2:
time: 45.8 us; the launch traced here: 44.9 us
  Pallas kernels  43.3 us (95%)
  local copies, waits for them, and re-layouts  1.57 us (3%)
    pallas_call x1, Pallas kernels, on_device(): pl.pallas_call(lambda f, e, o, *s: kernel(f, e, o, s), out_shape=jax.Shap...  43.3 us
    unnamed x1, local copies, waits for them, and re-layouts  1.57 us

profile of v2, /device:TPU:59, one launch (start us, length us, event | category | flops | bytes accessed | tf_op | source)
XLA Modules:
  0.0 44.9 jit_solution(929070630043894006)
XLA Ops:
  0.0 43.3 %shard_map.28 = f32[8,16,256]{2,1,0:T(8,128)} custom-call(f32[8,16,256]{2,1,0:T(8,128)} %f.1, f32[8,16,256]{2,1,0:T(8,128)} %e.1), custom_call_target="tpu_custom_call" | custom-call | tf_op jit(solution)/shard_map/pallas_call | solution.py:955
  43.4 1.6 %copy.4 = f32[8,16,256]{2,1,0:T(8,128)} copy(f32[8,16,256]{2,1,0:T(8,128)} %shard_map.28) | data formatting | bytes 262144
